TPU v7x, 32 devices: a whole 2x2x4 slice. The times are simulated.
32 devices in a mesh: grp: 2 (over x), sec: 16 (over z, y, core).
Axes of the slice: x: 2, y: 2, z: 4, core: 2. Of those that a mesh axis runs over, the one named last changes fastest.
Arguments:
- section_tile: bfloat16 [32, 512, 512], P(('grp', 'sec')), parts along dimension 0, may hold values from -8 to 8
- placement: int32 [64, 2], P('grp'), parts along dimension 0, may hold values from 0 to 384
- tissue_mask: int32 [32, 32], P(('grp', 'sec')), parts along dimension 0, may hold values 0 or 1
- level_use: int32 [3, 64], P(None, 'grp'), parts along dimension 1, may hold values 0 or 1
Outputs:
- flow_next: float32 [32, 2, 32], P(('grp', 'sec')), parts along dimension 0
- flow_skip: float32 [32, 2, 32], P(('grp', 'sec')), parts along dimension 0
- position: float32 [32, 2, 32], P(('grp', 'sec')), parts along dimension 0
There are 2 independent parts, one for each index of `grp`. A program takes and returns all parts, laid end to end along the dimension named above; each array names one. Nothing has to cross between parts.
All inputs are finite; a program needn't handle non-finite values. No bound on the sum of `tissue_mask` on one device may be relied on, other than what follows from the above.
Results may differ from a plain program's by a relative error of at most 0.0044.
Values may be sent and summed in bfloat16 or wider, within the bound.
A program may use at most 128 MiB of HBM per device.

v0:
```python
import jax
import jax.numpy as jnp
from jax import lax
from jax.sharding import PartitionSpec as P

PATCH = 128
LEVELS = 3


def passed_along(block, axis, distance):
    devices = range(lax.axis_size(axis))
    route = [(i - distance, i) for i in devices if i - distance in devices]
    return lax.ppermute(block, axis, route)


def entering(part, axis, combine, identity):
    place = lax.axis_index(axis)
    gathered = lax.all_gather(part, axis)
    state = jnp.zeros_like(part) + jnp.asarray(identity, part.dtype)

    def one(turn, state):
        return combine(state, lax.dynamic_index_in_dim(gathered, turn, 0, False))

    return lax.fori_loop(0, place, one, state)


def dft_tables():
    index = jnp.arange(PATCH, dtype=jnp.int32)
    product = index[:, None] * index[None, :] % PATCH
    angles = product.astype(jnp.float32) * (2.0 * jnp.pi / PATCH)
    return (jnp.cos(angles).astype(jnp.bfloat16), (-jnp.sin(angles)).astype(jnp.bfloat16))


def band_vector(level_number):
    index = jnp.arange(PATCH, dtype=jnp.int32)
    signed_freq = jnp.minimum(index, PATCH - index)
    return (signed_freq < PATCH // 2 ** (level_number + 1)).astype(jnp.bfloat16)


def offset_vector():
    index = jnp.arange(PATCH, dtype=jnp.int32)
    return jnp.where(index < PATCH // 2, index, index - PATCH).astype(jnp.float32)


def extract(plane, placement):

    def one_patch(corner):
        return lax.dynamic_slice(plane, (corner[0], corner[1]), (PATCH, PATCH))

    return jax.vmap(one_patch)(placement)


def matrix_product(form, left, right):
    return jnp.einsum(form, left, right, preferred_element_type=jnp.float32)


def spectrum(patches, cosine_lookup, sine_lookup):
    real_rows = matrix_product("kn,pnm->pkm", cosine_lookup, patches).astype(jnp.bfloat16)
    imag_rows = matrix_product("kn,pnm->pkm", sine_lookup, patches).astype(jnp.bfloat16)
    spec_real = (
        matrix_product("pkm,ml->pkl", real_rows, cosine_lookup)
        - matrix_product("pkm,ml->pkl", imag_rows, sine_lookup)
    ) / PATCH
    spec_imag = (
        matrix_product("pkm,ml->pkl", real_rows, sine_lookup)
        + matrix_product("pkm,ml->pkl", imag_rows, cosine_lookup)
    ) / PATCH
    return (spec_real.astype(jnp.bfloat16), spec_imag.astype(jnp.bfloat16))


def centroid(correl, offsets):
    weights = correl * correl
    total = jnp.sum(weights, axis=(1, 2)) + 1e-06
    along_rows = jnp.sum(weights * offsets[None, :, None], axis=(1, 2)) / total
    along_cols = jnp.sum(weights * offsets[None, None, :], axis=(1, 2)) / total
    return jnp.stack([along_rows, along_cols])


def pair_flow(own_real, own_imag, other_real, other_imag, cosine_lookup, sine_lookup, usage, valid):
    first_real = own_real.astype(jnp.float32)
    first_imag = own_imag.astype(jnp.float32)
    second_real = other_real.astype(jnp.float32)
    second_imag = other_imag.astype(jnp.float32)
    cross_power_real = (first_real * second_real + first_imag * second_imag).astype(jnp.bfloat16)
    cross_power_imaginary = (first_imag * second_real - first_real * second_imag).astype(
        jnp.bfloat16
    )
    offsets = offset_vector()
    estimate = jnp.zeros((2, usage.shape[1]), jnp.float32)
    for level_number in range(LEVELS):
        band_row = band_vector(level_number)
        cosine_left_factor = cosine_lookup * band_row[None, :]
        sine_left_factor = sine_lookup * band_row[None, :]
        cos_right = cosine_lookup * band_row[:, None]
        sin_right = sine_lookup * band_row[:, None]
        partial_real = (
            matrix_product("dt,hts->hds", cosine_left_factor, cross_power_real)
            + matrix_product("dt,hts->hds", sine_left_factor, cross_power_imaginary)
        ).astype(jnp.bfloat16)
        partial_imaginary = (
            matrix_product("dt,hts->hds", cosine_left_factor, cross_power_imaginary)
            - matrix_product("dt,hts->hds", sine_left_factor, cross_power_real)
        ).astype(jnp.bfloat16)
        correl = (
            matrix_product("pkq,ql->pkl", partial_real, cos_right)
            + matrix_product("pkq,ql->pkl", partial_imaginary, sin_right)
        ) / PATCH
        estimate = estimate + usage[level_number][None, :] * centroid(correl, offsets)
    count = jnp.maximum(jnp.sum(usage, axis=0), 1.0)
    return valid[None, :] * estimate / count[None, :]


def add_terms(earlier, later):
    return earlier + later


def on_device(section_tile, placement, tissue_mask, level_use):
    cosine_lookup, sine_lookup = dft_tables()
    own_real, own_imag = spectrum(extract(section_tile[0], placement), cosine_lookup, sine_lookup)
    own_flag = tissue_mask.astype(jnp.bfloat16)
    next_real, next_imag, next_flag = passed_along((own_real, own_imag, own_flag), "sec", -1)
    skip_real, skip_imag, skip_flag = passed_along((own_real, own_imag, own_flag), "sec", -2)
    usage = level_use.astype(jnp.float32)
    self_valid = tissue_mask[0].astype(jnp.float32)
    flow_next = pair_flow(
        own_real,
        own_imag,
        next_real,
        next_imag,
        cosine_lookup,
        sine_lookup,
        usage,
        self_valid * next_flag[0].astype(jnp.float32),
    )[None]
    flow_skip = pair_flow(
        own_real,
        own_imag,
        skip_real,
        skip_imag,
        cosine_lookup,
        sine_lookup,
        usage,
        self_valid * skip_flag[0].astype(jnp.float32),
    )[None]
    earlier = entering(flow_next, "sec", add_terms, jnp.zeros_like(flow_next))
    return (flow_next, flow_skip, earlier + flow_next)


def solution(mesh):
    in_specs = (
        P(("grp", "sec"), None, None),
        P("grp", None),
        P(("grp", "sec"), None),
        P(None, "grp"),
    )
    out_specs = (
        P(("grp", "sec"), None, None),
        P(("grp", "sec"), None, None),
        P(("grp", "sec"), None, None),
    )
    return jax.shard_map(
        on_device, mesh=mesh, in_specs=in_specs, out_specs=out_specs, check_vma=False
    )
```

profile of v0, /device:TPU:1, one launch (start us, length us, event | category | flops | bytes accessed | tf_op | source)
XLA Modules:
  0.0 277.0 jit_solution(1236571950580947353)
XLA Ops:
  1.4 92.6 %while.12 = (s32[]{:T(128)}, bf16[512,512]{1,0:T(8,128)(2,1)}, s32[32,2]{0,1:T(2,128)S(1)}, bf16[32,128,128]{2,1,0:T(8,128)(2,1)S(1)}, s32[]{:T(128)}) while((s32[]{:T(128)}, bf16[512,512]{1,0:T(8,128)(2,1)}, s32[32,2]{0,1:T(2,128)S(1)}, bf16[32,128,128]{2,1,0:T(8,128)(2,1)S(1)}, s32[]{:T(128)}) %tuple.89), condition=%wide.while_cond, body=%wide.while_body.sunk | while | flops 2 | bytes 65653 | solution.py:48
  2.0 2.3 bitcast_dynamic-update-slice_fusion.2
  4.9 2.3 bitcast_dynamic-update-slice_fusion.2
  7.8 2.3 bitcast_dynamic-update-slice_fusion.2
  10.7 2.3 bitcast_dynamic-update-slice_fusion.2
  13.6 2.3 bitcast_dynamic-update-slice_fusion.2
  16.5 2.3 bitcast_dynamic-update-slice_fusion.2
  19.4 2.3 bitcast_dynamic-update-slice_fusion.2
  22.3 2.3 bitcast_dynamic-update-slice_fusion.2
  25.2 2.3 bitcast_dynamic-update-slice_fusion.2
  28.1 2.3 bitcast_dynamic-update-slice_fusion.2
  31.0 2.3 bitcast_dynamic-update-slice_fusion.2
  33.9 2.3 bitcast_dynamic-update-slice_fusion.2
  36.8 2.3 bitcast_dynamic-update-slice_fusion.2
  39.7 2.3 bitcast_dynamic-update-slice_fusion.2
  42.6 2.3 bitcast_dynamic-update-slice_fusion.2
  45.5 2.3 bitcast_dynamic-update-slice_fusion.2
  48.4 2.3 bitcast_dynamic-update-slice_fusion.2
  51.3 2.3 bitcast_dynamic-update-slice_fusion.2
  54.2 2.3 bitcast_dynamic-update-slice_fusion.2
  57.0 2.3 bitcast_dynamic-update-slice_fusion.2
  59.9 2.3 bitcast_dynamic-update-slice_fusion.2
  65.7 2.3 bitcast_dynamic-update-slice_fusion.2
  68.6 2.3 bitcast_dynamic-update-slice_fusion.2
  71.5 2.3 bitcast_dynamic-update-slice_fusion.2
  74.4 2.3 bitcast_dynamic-update-slice_fusion.2
  77.3 2.3 bitcast_dynamic-update-slice_fusion.2
  80.2 2.3 bitcast_dynamic-update-slice_fusion.2
  83.1 2.3 bitcast_dynamic-update-slice_fusion.2
  86.0 2.3 bitcast_dynamic-update-slice_fusion.2
  88.9 2.3 bitcast_dynamic-update-slice_fusion.2
  106.2 43.3 %collective-permute-done.3 = bf16[1,32]{1,0:T(2,128)(2,1)S(1)} collective-permute-done((bf16[1,32]{1,0:T(2,128)(2,1)S(1)}, bf16[1,32]{1,0:T(2,128)(2,1)S(1)}, u32[]{:S(2)}, u32[]{:S(2)}) %collective-permute-start.3) | collective-permute-done | bytes 96 | tf_op jit(solution)/shard_map/ppermute | solution.py:13
  149.4 23.4 %collective-permute-start = (bf16[1,32]{1,0:T(2,128)(2,1)S(1)}, bf16[1,32]{1,0:T(2,128)(2,1)S(1)}, u32[]{:S(2)}, u32[]{:S(2)}) collective-permute-start(bf16[1,32]{1,0:T(2,128)(2,1)S(1)} %convert_element_type.449), channel_id=1, source_target_pairs={{1,0},{2,1},{3,2},{4,3},{5,4},{6,5},{7,6},{8,7},{9,8},{10,9},{11,1... | collective-permute-start | bytes 200 | tf_op jit(solution)/shard_map/ppermute | solution.py:13
  172.9 3.0 %collective-permute-done = bf16[1,32]{1,0:T(2,128)(2,1)S(1)} collective-permute-done((bf16[1,32]{1,0:T(2,128)(2,1)S(1)}, bf16[1,32]{1,0:T(2,128)(2,1)S(1)}, u32[]{:S(2)}, u32[]{:S(2)}) %collective-permute-start) | collective-permute-done | bytes 96 | tf_op jit(solution)/shard_map/ppermute | solution.py:13
  176.9 4.3 %fusion.1 = (bf16[32,128,128]{2,1,0:T(8,128)(2,1)S(1)}, bf16[32,128,128]{2,1,0:T(8,128)(2,1)S(1)}, bf16[32,128,128]{2,1,0:T(8,128)(2,1)S(1)}, bf16[32,128,128]{2,1,0:T(8,128)(2,1)S(1)}) fusion(bf16[32,128,128]{2,1,0:T(8,128)(2,1)} %collective-permute-done.1, bf16[32,128,128]{2,1,0:T(8,128)(2,1)} %copy-done.3, bf16[32,128,128]{2,1,0:T(8,128)(2,1)} %copy-done.4, ...), kind=kLoop, calls=%fused_computation.12 | loop fusion | flops 11534336 | bytes 10485760 | tf_op jit(solution)/shard_map/convert_element_type | solution.py:84
  205.2 3.9 %fusion.14 = f32[32,128,128]{2,1,0:T(8,128)} fusion(f32[32,128,128]{1,2,0:T(8,128)} %fusion.58, bf16[32,128,128]{2,1,0:T(8,128)(2,1)S(1)} %get-tuple-element.88, bf16[128]{0:T(256)(128)(2,1)S(1)} %compare_convert_fusion.1), kind=kOutput, calls=%fused_computation.59 | convolution fusion | flops 270106624 | bytes 5243136 | tf_op jit(solution)/shard_map/pkq,ql->pkl/dot_general | solution.py:54
  209.1 3.9 %fusion.17 = f32[32,128,128]{2,1,0:T(8,128)} fusion(f32[32,128,128]{1,2,0:T(8,128)} %fusion.38, bf16[32,128,128]{2,1,0:T(8,128)(2,1)S(1)} %get-tuple-element.88, bf16[128]{0:T(256)(128)(2,1)S(1)} %compare_convert_fusion), kind=kOutput, calls=%fused_computation.62 | convolution fusion | flops 270106624 | bytes 5243136 | tf_op jit(solution)/shard_map/pkq,ql->pkl/dot_general | solution.py:54
  212.9 3.9 %fusion.23 = f32[32,128,128]{2,1,0:T(8,128)} fusion(f32[32,128,128]{1,2,0:T(8,128)} %fusion.62, bf16[32,128,128]{2,1,0:T(8,128)(2,1)S(1)} %get-tuple-element.93, bf16[128]{0:T(256)(128)(2,1)S(1)} %compare_convert_fusion.1), kind=kOutput, calls=%fused_computation.68 | convolution fusion | flops 270106624 | bytes 5243136 | tf_op jit(solution)/shard_map/pkq,ql->pkl/dot_general | solution.py:54
  216.9 3.8 %fusion.26 = f32[32,128,128]{2,1,0:T(8,128)} fusion(f32[32,128,128]{1,2,0:T(8,128)} %fusion.42, bf16[32,128,128]{2,1,0:T(8,128)(2,1)S(1)} %get-tuple-element.93, bf16[128]{0:T(256)(128)(2,1)S(1)} %compare_convert_fusion), kind=kOutput, calls=%fused_computation.71 | convolution fusion | flops 270106624 | bytes 5243136 | tf_op jit(solution)/shard_map/pkq,ql->pkl/dot_general | solution.py:54
  220.7 4.1 %fusion.11 = f32[32,128,128]{2,1,0:T(8,128)} fusion(f32[32,128,128]{1,2,0:T(8,128)} %fusion.78, bf16[32,128,128]{2,1,0:T(8,128)(2,1)S(1)} %get-tuple-element.88, bf16[128]{0:T(256)(128)(2,1)S(1)} %compare_convert_fusion.2), kind=kOutput, calls=%fused_computation.56 | convolution fusion | flops 270106624 | bytes 5243136 | tf_op jit(solution)/shard_map/pkq,ql->pkl/dot_general | solution.py:54
  224.8 3.9 %fusion.20 = f32[32,128,128]{2,1,0:T(8,128)} fusion(f32[32,128,128]{1,2,0:T(8,128)} %fusion.82, bf16[32,128,128]{2,1,0:T(8,128)(2,1)S(1)} %get-tuple-element.93, bf16[128]{0:T(256)(128)(2,1)S(1)} %compare_convert_fusion.2), kind=kOutput, calls=%fused_computation.65 | convolution fusion | flops 270106624 | bytes 5243136 | tf_op jit(solution)/shard_map/pkq,ql->pkl/dot_general | solution.py:54
  228.7 4.5 %multiply_multiply_fusion.4 = f32[32,128,128]{2,1,0:T(8,128)} fusion(f32[32,128,128]{2,1,0:T(8,128)} %fusion.14, f32[32,128,128]{1,2,0:T(8,128)} %fusion.60, bf16[32,128,128]{2,1,0:T(8,128)(2,1)S(1)} %get-tuple-element.89, bf16[128]{0:T(256)(128)(2,1)S(1)} %compare_convert_fusion.1), kind=kOutput, calls=%fused_computation.41 | convolution fusion | flops 271695872 | bytes 7340288 | tf_op jit(solution)/shard_map/pkq,ql->pkl/dot_general | solution.py:54
  233.2 4.6 %multiply_multiply_fusion.3 = f32[32,128,128]{2,1,0:T(8,128)} fusion(f32[32,128,128]{2,1,0:T(8,128)} %fusion.17, f32[32,128,128]{1,2,0:T(8,128)} %fusion.40, bf16[32,128,128]{2,1,0:T(8,128)(2,1)S(1)} %get-tuple-element.89, bf16[128]{0:T(256)(128)(2,1)S(1)} %compare_convert_fusion), kind=kOutput, calls=%fused_computation.36 | convolution fusion | flops 271695872 | bytes 7340288 | tf_op jit(solution)/shard_map/pkq,ql->pkl/dot_general | solution.py:54
  237.8 4.6 %multiply_multiply_fusion.1 = f32[32,128,128]{2,1,0:T(8,128)} fusion(f32[32,128,128]{2,1,0:T(8,128)} %fusion.23, f32[32,128,128]{1,2,0:T(8,128)} %fusion.64, bf16[32,128,128]{2,1,0:T(8,128)(2,1)S(1)} %copy-done.1, bf16[128]{0:T(256)(128)(2,1)S(1)} %compare_convert_fusion.1), kind=kOutput, calls=%fused_computation.26 | convolution fusion | flops 271695872 | bytes 7340288 | tf_op jit(solution)/shard_map/pkq,ql->pkl/dot_general | solution.py:54
  242.4 4.5 %multiply_multiply_fusion = f32[32,128,128]{2,1,0:T(8,128)} fusion(f32[32,128,128]{2,1,0:T(8,128)} %fusion.26, f32[32,128,128]{1,2,0:T(8,128)} %fusion.44, bf16[32,128,128]{2,1,0:T(8,128)(2,1)S(1)} %copy-done.1, bf16[128]{0:T(256)(128)(2,1)S(1)} %compare_convert_fusion), kind=kOutput, calls=%fused_computation.21 | convolution fusion | flops 271695872 | bytes 7340288 | tf_op jit(solution)/shard_map/pkq,ql->pkl/dot_general | solution.py:54
  246.8 4.5 %multiply_multiply_fusion.5 = f32[32,128,128]{2,1,0:T(8,128)} fusion(f32[32,128,128]{2,1,0:T(8,128)} %fusion.11, f32[32,128,128]{1,2,0:T(8,128)} %fusion.80, bf16[32,128,128]{2,1,0:T(8,128)(2,1)S(1)} %get-tuple-element.89, bf16[128]{0:T(256)(128)(2,1)S(1)} %compare_convert_fusion.2), kind=kOutput, calls=%fused_computation.46 | convolution fusion | flops 271695872 | bytes 7340288 | tf_op jit(solution)/shard_map/pkq,ql->pkl/dot_general | solution.py:54
  251.3 7.3 %multiply_reduce_fusion.5 = (f32[32]{0:T(128)S(1)}, f32[32]{0:T(128)S(1)}, f32[32]{0:T(128)S(1)}, f32[32]{0:T(128)S(1)}, f32[32]{0:T(128)S(1)}, /*index=5*/f32[3...) fusion(f32[128]{0:T(128)S(1)} %fusion.222, ...), kind=kOutput, calls=%fused_computation.30 | convolution fusion | flops 287423936 | bytes 15731712 | tf_op jit(solution)/shard_map/pkq,ql->pkl/dot_general | solution.py:54
  258.7 17.6 %all_gather.3 = f32[16,1,2,32]{3,2,1,0:T(2,128)S(1)} all-gather(f32[1,1,2,32]{3,2,1,0:T(2,128)S(1)} %fusion.219), channel_id=1, replica_groups=mesh['grp'=2,'sec'=16] {'sec'}, dimensions={0}, use_global_device_ids=true | all-gather | bytes 4352 | tf_op jit(solution)/shard_map/all_gather | solution.py:18
  (129 shorter events, 61.9 us)
Async XLA Ops:
  96.8 4.7 %copy-start.2 = (bf16[32,128,128]{2,1,0:T(8,128)(2,1)}, bf16[32,128,128]{2,1,0:T(8,128)(2,1)S(1)}, u32[]{:S(2)}) copy-start(bf16[32,128,128]{2,1,0:T(8,128)(2,1)S(1)} %multiply_convert_fusion) | copy-start | bytes 3145732
  96.8 79.1 %collective-permute-start.2 = (bf16[32,128,128]{2,1,0:T(8,128)(2,1)S(1)}, bf16[32,128,128]{2,1,0:T(8,128)(2,1)S(1)}, u32[]{:S(2)}, u32[]{:S(2)}) collective-permute-start(bf16[32,128,128]{2,1,0:T(8,128)(2,1)S(1)} %multiply_convert_fusion), channel_id=1, source_target_pairs={{1,0},{2,1},{3,2},{4,3},{5,4},{6,5},{7,6},{8,7},{9,8},{10,9},{11,1... | collective-permute-start | bytes 3145736 | tf_op jit(solution)/shard_map/ppermute | solution.py:13
  98.8 77.1 %collective-permute-start.5 = (bf16[32,128,128]{2,1,0:T(8,128)(2,1)S(1)}, bf16[32,128,128]{2,1,0:T(8,128)(2,1)}, u32[]{:S(2)}, u32[]{:S(2)}) collective-permute-start(bf16[32,128,128]{2,1,0:T(8,128)(2,1)S(1)} %multiply_convert_fusion), channel_id=1, source_target_pairs={{2,0},{3,1},{4,2},{5,3},{6,4},{7,5},{8,6},{9,7},{10,8},{11,9},{12,... | collective-permute-start | bytes 3145736 | tf_op jit(solution)/shard_map/ppermute | solution.py:13
  100.8 4.0 %copy-start.6 = (s32[1,32]{1,0:T(1,128)S(1)}, s32[1,32]{1,0:T(1,128)}, u32[]{:S(2)}) copy-start(s32[1,32]{1,0:T(1,128)} %param.8) | copy-start | bytes 388
  100.8 5.3 %copy-start.5 = (s32[3,32]{1,0:T(4,128)S(1)}, s32[3,32]{1,0:T(4,128)}, u32[]{:S(2)}) copy-start(s32[3,32]{1,0:T(4,128)} %param.9) | copy-start | bytes 1156
  101.5 74.4 %copy-start.3 = (bf16[32,128,128]{2,1,0:T(8,128)(2,1)}, bf16[32,128,128]{2,1,0:T(8,128)(2,1)S(1)}, u32[]{:S(2)}) copy-start(bf16[32,128,128]{2,1,0:T(8,128)(2,1)S(1)} %multiply_convert_fusion.1) | copy-start | bytes 3145732
  101.5 74.4 %collective-permute-start.1 = (bf16[32,128,128]{2,1,0:T(8,128)(2,1)S(1)}, bf16[32,128,128]{2,1,0:T(8,128)(2,1)}, u32[]{:S(2)}, u32[]{:S(2)}) collective-permute-start(bf16[32,128,128]{2,1,0:T(8,128)(2,1)S(1)} %multiply_convert_fusion.1), channel_id=1, source_target_pairs={{1,0},{2,1},{3,2},{4,3},{5,4},{6,5},{7,6},{8,7},{9,8},{10,9},{11,1... | collective-permute-start | bytes 3145736 | tf_op jit(solution)/shard_map/ppermute | solution.py:13
  103.5 73.4 %collective-permute-start.4 = (bf16[32,128,128]{2,1,0:T(8,128)(2,1)S(1)}, bf16[32,128,128]{2,1,0:T(8,128)(2,1)}, u32[]{:S(2)}, u32[]{:S(2)}) collective-permute-start(bf16[32,128,128]{2,1,0:T(8,128)(2,1)S(1)} %multiply_convert_fusion.1), channel_id=1, source_target_pairs={{2,0},{3,1},{4,2},{5,3},{6,4},{7,5},{8,6},{9,7},{10,8},{11,9},{12,... | collective-permute-start | bytes 3145736 | tf_op jit(solution)/shard_map/ppermute | solution.py:13
  104.8 44.7 %collective-permute-start.3 = (bf16[1,32]{1,0:T(2,128)(2,1)S(1)}, bf16[1,32]{1,0:T(2,128)(2,1)S(1)}, u32[]{:S(2)}, u32[]{:S(2)}) collective-permute-start(bf16[1,32]{1,0:T(2,128)(2,1)S(1)} %convert_element_type.449), channel_id=1, source_target_pairs={{2,0},{3,1},{4,2},{5,3},{6,4},{7,5},{8,6},{9,7},{10,8},{11,9},{12,... | collective-permute-start | bytes 200 | tf_op jit(solution)/shard_map/ppermute | solution.py:13
  149.4 26.4 %collective-permute-start = (bf16[1,32]{1,0:T(2,128)(2,1)S(1)}, bf16[1,32]{1,0:T(2,128)(2,1)S(1)}, u32[]{:S(2)}, u32[]{:S(2)}) collective-permute-start(bf16[1,32]{1,0:T(2,128)(2,1)S(1)} %convert_element_type.449), channel_id=1, source_target_pairs={{1,0},{2,1},{3,2},{4,3},{5,4},{6,5},{7,6},{8,7},{9,8},{10,9},{11,1... | collective-permute-start | bytes 200 | tf_op jit(solution)/shard_map/ppermute | solution.py:13
  175.9 1.0 copy-start.4
  181.2 20.1 %copy-start = (bf16[32,128,128]{2,1,0:T(8,128)(2,1)}, bf16[32,128,128]{2,1,0:T(8,128)(2,1)S(1)}, u32[]{:S(2)}) copy-start(bf16[32,128,128]{2,1,0:T(8,128)(2,1)S(1)} %get-tuple-element.92) | copy-start | bytes 3145732
  233.2 4.6 %copy-start.1 = (bf16[32,128,128]{2,1,0:T(8,128)(2,1)S(1)}, bf16[32,128,128]{2,1,0:T(8,128)(2,1)}, u32[]{:S(2)}) copy-start(bf16[32,128,128]{2,1,0:T(8,128)(2,1)} %copy-done) | copy-start | bytes 3145732
where the time goes:
time: 280 us; the launch traced here: 277 us
  local copies, waits for them, and re-layouts  93.1 us (33%)
  matrix products  81.5 us (29%)
  waiting for transfers between devices  46.3 us (17%)
  starting transfers between devices  31.2 us (11%)
  blocking collectives  17.6 us (6%)
  other arithmetic  5.78 us (2%)
    gather x96, local copies, waits for them, and re-layouts  92.1 us
    dot_general x30, matrix products, matrix_product(): return jnp.einsum(form, left, right, preferred_element_type=jnp.float32)  81.5 us
    ppermute x6, waiting for transfers between devices, passed_along(): return lax.ppermute(block, axis, route)  46.3 us
    ppermute x6, starting transfers between devices, passed_along(): return lax.ppermute(block, axis, route)  31.2 us
    all_gather x1, blocking collectives, entering(): gathered = lax.all_gather(part, axis)  17.6 us
  transfers between devices with their start and end apart: 6, of which 2 were waited for; matrix products, arithmetic and copies ran while one was open for 1% of the time, Pallas kernels for 0%

commit v1 on v0

v1 whole, which is shorter than its diff:
```python
import functools

import jax
import jax.numpy as jnp
import ml_dtypes
import numpy as np
from jax import lax
from jax.experimental import pallas as pl
from jax.experimental.pallas import tpu as pltpu
from jax.sharding import PartitionSpec as P

PATCH = 128
HALF = PATCH // 2
LEVELS = 3
MESH = pl.DeviceIdType.MESH


def tables():
    index = np.arange(PATCH)
    product = (index[:, None] * index[None, :]) % PATCH
    angles = product.astype(np.float32) * np.float32(2.0 * np.pi / PATCH)
    cos = np.cos(angles).astype(ml_dtypes.bfloat16).astype(np.float32)
    sin = (-np.sin(angles)).astype(ml_dtypes.bfloat16).astype(np.float32)

    rows = np.concatenate([cos[:HALF], sin[:HALF]], axis=0)

    def two(block):
        zero = np.zeros_like(block)
        return np.block([[block, zero], [zero, block]])

    c, s = cos[:, :HALF] / PATCH, sin[:, :HALF] / PATCH
    cols = np.stack(
        [np.concatenate([two(c), two(s)], 1), np.concatenate([two(-s), two(c)], 1)]
    )

    freq = np.concatenate([np.arange(HALF), (-np.arange(HALF)) % PATCH])
    used = (np.arange(PATCH) != HALF).astype(np.float32)
    first, second = [], []
    for level in range(LEVELS):
        band = (np.arange(HALF) < PATCH // 2 ** (level + 1)).astype(np.float32)
        keep = np.concatenate([band, band]) * used
        c, s = cos[:, freq] * keep, sin[:, freq] * keep
        first.append(np.block([[c, s], [-s, c]]))
        weight = (np.where(np.arange(HALF) == 0, 1.0, 2.0) / PATCH * band)[:, None]
        second.append(
            np.concatenate([two(cos[:HALF] * weight), two(sin[:HALF] * weight)], 0)
        )
    first = np.concatenate(first, 0)
    second = np.stack(second)
    return tuple(t.astype(ml_dtypes.bfloat16) for t in (rows, cols, first, second))


def dot(a, b):
    return jnp.dot(a, b, preferred_element_type=jnp.float32)


def centre(position):
    return 8 * position if 8 * position < HALF else 8 * position - PATCH


def kernel(
    n, tile_ref, place_ref, mask_ref, use_ref, rows_ref, cols_ref, first_ref, second_ref,
    next_ref, skip_ref, pos_ref,
    wide, got, got_mask, own, totals, moments, mine, earlier,
    tile_send, tile_recv, mask_send, mask_recv, flow_send, flow_recv,
):
    me = lax.axis_index("sec")
    grp = lax.axis_index("grp")
    patches = use_ref.shape[1]
    pairs = patches // 2
    side = tile_ref.shape[1]

    barrier = pltpu.get_barrier_semaphore()

    def greet(step, _):
        other = lax.rem(me + step, n)
        pl.semaphore_signal(barrier, inc=1, device_id=(grp, other), device_id_type=MESH)
        return 0

    lax.fori_loop(1, n, greet, 0)
    pl.semaphore_wait(barrier, n - 1)

    def tile_copy(gap):
        return pltpu.make_async_remote_copy(
            src_ref=tile_ref.at[0], dst_ref=got.at[gap - 1],
            send_sem=tile_send.at[gap - 1], recv_sem=tile_recv.at[gap - 1],
            device_id=(grp, me - gap), device_id_type=MESH,
        )

    def mask_copy(gap):
        return pltpu.make_async_remote_copy(
            src_ref=mask_ref, dst_ref=got_mask.at[gap - 1],
            send_sem=mask_send.at[gap - 1], recv_sem=mask_recv.at[gap - 1],
            device_id=(grp, me - gap), device_id_type=MESH,
        )

    for gap in (1, 2):
        @pl.when(me >= gap)
        def _(gap=gap):
            tile_copy(gap).start()
            mask_copy(gap).start()

    lane = lax.broadcasted_iota(jnp.int32, (PATCH, PATCH), 1)

    def patch(p):
        row, col = place_ref[p, 0], place_ref[p, 1]
        block = lax.div(col, PATCH)
        within = lax.rem(col, PATCH)
        a = wide[block, pl.ds(row, PATCH), :]
        b = wide[jnp.minimum(block + 1, side // PATCH - 1), pl.ds(row, PATCH), :]
        mixed = jnp.where(lane >= within, a, b)
        shift = lax.rem(PATCH - within, PATCH)
        return pltpu.roll(mixed, shift, 1).astype(jnp.bfloat16)

    def spectra(q):
        halves = []
        for pair in (q, q + 1):
            both = jnp.concatenate([patch(pair), patch(pair + pairs)], axis=1)
            halves.append(dot(rows_ref[...], both).astype(jnp.bfloat16))
        u = dot(jnp.concatenate([h[:HALF] for h in halves], 0), cols_ref[0])
        v = dot(jnp.concatenate([h[HALF:] for h in halves], 0), cols_ref[1])
        plus, minus = (u + v).astype(jnp.bfloat16), (u - v).astype(jnp.bfloat16)
        return [
            jnp.concatenate([plus[HALF * i:HALF * (i + 1)], minus[HALF * i:HALF * (i + 1)]], 0)
            for i in (0, 1)
        ]

    def own_quad(i, _):
        for j, value in enumerate(spectra(2 * i)):
            own[2 * i + j] = value
        return 0

    sub = lax.broadcasted_iota(jnp.int32, (8, 2 * PATCH), 0).astype(jnp.float32)

    def pair_quad(i, _):
        q = 2 * i
        real, imag = [], []
        for j, other in enumerate(spectra(q)):
            mine_ = own[q + j].astype(jnp.float32)
            other = other.astype(jnp.float32)
            ar, ai = mine_[:, :PATCH], mine_[:, PATCH:]
            br, bi = other[:, :PATCH], other[:, PATCH:]
            real.append((ar * br + ai * bi).astype(jnp.bfloat16))
            imag.append((ai * br - ar * bi).astype(jnp.bfloat16))
        cross = jnp.concatenate(
            [jnp.concatenate(real, 1), jnp.concatenate(imag, 1)], 0
        )
        for level in range(LEVELS):
            half = dot(
                first_ref[pl.ds(2 * PATCH * level, 2 * PATCH)], cross
            ).astype(jnp.bfloat16)
            for j in (0, 1):
                lanes = slice(PATCH * j, PATCH * (j + 1))
                both = jnp.concatenate([half[:PATCH, lanes], half[PATCH:, lanes]], 1)
                correl = dot(both, second_ref[level])
                weights = correl * correl
                total = jnp.zeros((8, 2 * PATCH), jnp.float32)
                moment = jnp.zeros((8, 2 * PATCH), jnp.float32)
                for g in range(PATCH // 8):
                    w = weights[8 * g:8 * (g + 1)]
                    total = total + w
                    if centre(g):
                        moment = moment + w * float(centre(g))
                moment = moment + sub * total
                total = jnp.sum(total, 0, keepdims=True)
                moment = jnp.sum(moment, 0, keepdims=True)
                for h in (0, 1):
                    lanes_ = slice(PATCH * h, PATCH * (h + 1))
                    totals[level, pl.ds(q + j + h * pairs, 1), :] = total[:, lanes_]
                    moments[level, pl.ds(q + j + h * pairs, 1), :] = moment[:, lanes_]
        return 0

    position = lax.broadcasted_iota(jnp.int32, (8, PATCH), 1)
    offset = jnp.where(position < HALF, position, position - PATCH).astype(jnp.float32)
    which = lax.broadcasted_iota(jnp.int32, (8, PATCH), 0)
    gather = jnp.where(which == 0, 1.0, jnp.where(which == 1, offset, 0.0))

    def over_lanes(values):
        return lax.dot_general(
            gather, values, (((1,), (1,)), ((), ())),
            precision=lax.Precision.HIGHEST, preferred_element_type=jnp.float32,
        )

    def flow(gap):
        usage = use_ref[...].astype(jnp.float32)
        along_rows = jnp.zeros((1, patches), jnp.float32)
        along_cols = jnp.zeros((1, patches), jnp.float32)
        for level in range(LEVELS):
            whole = over_lanes(totals[level])
            slope = over_lanes(moments[level])
            use = usage[level:level + 1]
            norm = whole[0:1] + 1e-06
            along_rows = along_rows + use * (slope[0:1] / norm)
            along_cols = along_cols + use * (whole[1:2] / norm)
        count = jnp.maximum(jnp.sum(usage, axis=0, keepdims=True), 1.0)
        valid = mask_ref[...].astype(jnp.float32) * got_mask[gap - 1].astype(jnp.float32)
        both = jnp.concatenate([along_rows, along_cols], 0)
        return valid * both / count

    def widen(plane):
        for block in range(side // PATCH):
            lanes = pl.ds(PATCH * block, PATCH)
            wide[block] = plane[:, lanes].astype(jnp.float32)

    widen(tile_ref.at[0])
    lax.fori_loop(0, pairs // 2, own_quad, 0)

    def flow_copy(other):
        return pltpu.make_async_remote_copy(
            src_ref=mine, dst_ref=earlier.at[me],
            send_sem=flow_send.at[other], recv_sem=flow_recv.at[me],
            device_id=(grp, other), device_id_type=MESH,
        )

    for gap, out in ((1, next_ref), (2, skip_ref)):
        @pl.when(me + gap < n)
        def _(gap=gap, out=out):
            tile_copy(gap).wait_recv()
            mask_copy(gap).wait_recv()
            widen(got.at[gap - 1])
            lax.fori_loop(0, pairs // 2, pair_quad, 0)
            out[0] = flow(gap)

        @pl.when(me + gap >= n)
        def _(out=out):
            out[...] = jnp.zeros_like(out)

        if gap == 1:
            mine[...] = out[0]

            def send(other, _):
                flow_copy(other).start()
                return 0

            lax.fori_loop(me + 1, n, send, 0)

    def arrived(t, state):
        pltpu.make_async_remote_copy(
            src_ref=mine, dst_ref=earlier.at[t],
            send_sem=flow_send.at[t], recv_sem=flow_recv.at[t],
            device_id=(grp, me), device_id_type=MESH,
        ).wait_recv()
        return state + earlier[t]

    before = lax.fori_loop(0, me, arrived, jnp.zeros(mine.shape, jnp.float32))
    pos_ref[0] = before + mine[...]

    def sent(other, _):
        flow_copy(other).wait_send()
        return 0

    lax.fori_loop(me + 1, n, sent, 0)
    for gap in (1, 2):
        @pl.when(me >= gap)
        def _(gap=gap):
            tile_copy(gap).wait_send()
            mask_copy(gap).wait_send()


def on_device(n, section_tile, placement, tissue_mask, level_use):
    side = section_tile.shape[1]
    patches = placement.shape[0]
    out = jax.ShapeDtypeStruct((1, 2, patches), jnp.float32)
    vmem = pl.BlockSpec(memory_space=pltpu.VMEM)
    smem = pl.BlockSpec(memory_space=pltpu.SMEM)
    dma = pltpu.SemaphoreType.DMA
    return pl.pallas_call(
        functools.partial(kernel, n),
        out_shape=(out, out, out),
        in_specs=[vmem, smem] + [vmem] * 6,
        out_specs=(vmem, vmem, vmem),
        scratch_shapes=[
            pltpu.VMEM((side // PATCH, side, PATCH), jnp.float32),
            pltpu.VMEM((2, side, side), jnp.bfloat16),
            pltpu.VMEM((2, 1, patches), jnp.int32),
            pltpu.VMEM((patches // 2, PATCH, 2 * PATCH), jnp.bfloat16),
            pltpu.VMEM((LEVELS, patches, PATCH), jnp.float32),
            pltpu.VMEM((LEVELS, patches, PATCH), jnp.float32),
            pltpu.VMEM((2, patches), jnp.float32),
            pltpu.VMEM((n, 2, patches), jnp.float32),
            dma((2,)), dma((2,)), dma((2,)), dma((2,)), dma((n,)), dma((n,)),
        ],
        compiler_params=pltpu.CompilerParams(
            collective_id=0, has_side_effects=True, vmem_limit_bytes=40 * 2**20
        ),
    )(section_tile, placement, tissue_mask, level_use, *[jnp.asarray(t) for t in tables()])


def solution(mesh):
    in_specs = (
        P(("grp", "sec"), None, None),
        P("grp", None),
        P(("grp", "sec"), None),
        P(None, "grp"),
    )
    out_specs = (P(("grp", "sec"), None, None),) * 3
    return jax.shard_map(
        functools.partial(on_device, mesh.shape["sec"]),
        mesh=mesh, in_specs=in_specs, out_specs=out_specs, check_vma=False,
    )
```

time: 280 us -> 43.6 us (0.16)
  local copies, waits for them, and re-layouts: 93.1 us -> 7.2 us
  matrix products: 81.5 us -> 0 us
  waiting for transfers between devices: 46.3 us -> 0 us
  Pallas kernels: 0 us -> 35.3 us
  starting transfers between devices: 31.2 us -> 0 us
  blocking collectives: 17.6 us -> 0 us
  other arithmetic: 5.78 us -> 0 us
    gather x96 -> x0, local copies, waits for them, and re-layouts: 92.1 us -> none
    dot_general x30 -> x0, matrix products: 81.5 us -> none  [matrix_product(): return jnp.einsum(form, left, right, preferred_element_type=jnp.float32)]
    ppermute x6 -> x0, waiting for transfers between devices: 46.3 us -> none  [passed_along(): return lax.ppermute(block, axis, route)]
    pallas_call x0 -> x1, Pallas kernels: none -> 35.3 us  [on_device(): pl.pallas_call(functools.partial(kernel, n), out_shape=(out, out, out), i...]
    ppermute x6 -> x0, starting transfers between devices: 31.2 us -> none  [passed_along(): return lax.ppermute(block, axis, route)]
    all_gather x1 -> x0, blocking collectives: 17.6 us -> none  [entering(): gathered = lax.all_gather(part, axis)]
    unnamed x14 -> x18, local copies, waits for them, and re-layouts: 0.99 us -> 7.2 us
    convert_element_type x7 -> x0, other arithmetic: 4.33 us -> none  [the longest x1 4.3 us: pair_flow(): (first_real * second_real + first_imag * second_imag).astype(jnp.bfloat16)]
  transfers between devices with their start and end apart: 6 -> 0, of which waited for: 2 -> 0; matrix products, arithmetic and copies ran while one was open for 1% -> 0% of each run, Pallas kernels for 0% -> 0%
where the time goes in v1:
time: 43.6 us; the launch traced here: 43.2 us
  Pallas kernels  35.3 us (81%)
  local copies, waits for them, and re-layouts  7.2 us (17%)
  between operations  0.67 us (2%)
    pallas_call x1, Pallas kernels, on_device(): pl.pallas_call(functools.partial(kernel, n), out_shape=(out, out, out), i...  35.3 us
    unnamed x18, local copies, waits for them, and re-layouts  7.2 us

profile of v1, /device:TPU:1, one launch (start us, length us, event | category | flops | bytes accessed | tf_op | source)
XLA Modules:
  0.0 43.2 jit_solution(2672852933706221543)
XLA Ops:
  0.6 0.0 copy-start.5
  0.6 0.0 copy-start.6
  0.7 0.8 %copy.11.place_ref = s32[32,2]{1,0:T(8,128)S(1)} copy(s32[32,2]{0,1:T(2,128)} %param.9) | data formatting | bytes 512 | tf_op args[1]
  1.4 0.0 copy-done.5
  1.4 0.0 copy-done.6
  1.4 0.0 copy-start
  1.4 1.0 %copy-done = bf16[1,512,512]{2,1,0:T(8,128)(2,1)S(1)} copy-done((bf16[1,512,512]{2,1,0:T(8,128)(2,1)S(1)}, bf16[1,512,512]{2,1,0:T(8,128)(2,1)}, u32[]{:S(2)}) %copy-start) | copy-done | bytes 524312
  2.5 0.0 copy-start.1
  2.5 1.0 %copy-done.1 = bf16[3,256,256]{2,1,0:T(8,128)(2,1)S(1)} copy-done((bf16[3,256,256]{2,1,0:T(8,128)(2,1)S(1)}, bf16[3,256,256]{2,1,0:T(8,128)(2,1)}, u32[]{:S(2)}) %copy-start.1) | copy-done | bytes 393240
  3.5 0.0 copy-start.2
  3.5 1.0 %copy-done.2 = bf16[768,256]{1,0:T(8,128)(2,1)S(1)} copy-done((bf16[768,256]{1,0:T(8,128)(2,1)S(1)}, bf16[768,256]{1,0:T(8,128)(2,1)}, u32[]{:S(2)}) %copy-start.2) | copy-done | bytes 393240
  4.5 0.0 copy-start.3
  4.5 0.9 %copy-done.3 = bf16[2,256,256]{2,1,0:T(8,128)(2,1)S(1)} copy-done((bf16[2,256,256]{2,1,0:T(8,128)(2,1)S(1)}, bf16[2,256,256]{2,1,0:T(8,128)(2,1)}, u32[]{:S(2)}) %copy-start.3) | copy-done | bytes 262168
  5.4 0.0 copy-start.4
  5.4 0.8 %copy-done.4 = bf16[128,128]{1,0:T(8,128)(2,1)S(1)} copy-done((bf16[128,128]{1,0:T(8,128)(2,1)S(1)}, bf16[128,128]{1,0:T(8,128)(2,1)}, u32[]{:S(2)}) %copy-start.4) | copy-done | bytes 32792
  6.2 35.3 %shard_map.103 = (f32[1,2,32]{2,1,0:T(2,128)S(1)}, f32[1,2,32]{2,1,0:T(2,128)S(1)}, f32[1,2,32]{2,1,0:T(2,128)S(1)}) custom-call(bf16[1,512,512]{2,1,0:T(8,128)(2,1)S(1)} %copy-done, s32[32,2]{1,0:T(8,128)S(1)} %copy.11.place_ref, s32[1,32]{1,0:T(1,128)S(1)} %copy-done.6, s32[3,32]{1,0:T(4,128)S(1)} %copy-done.5, bf16[128,128]{1,0:T(8,128)(2,1)S(1)} %copy-done.4, ...), custom_call_target="tpu_custom_call" | custom-call | tf_op jit(solution)/shard_map/pallas_call | solution.py:267
  41.5 0.6 %copy.15 = f32[1,2,32]{2,1,0:T(2,128)} copy(f32[1,2,32]{2,1,0:T(2,128)S(1)} %get-tuple-element.6) | data formatting | bytes 512
  42.1 0.6 %copy.16 = f32[1,2,32]{2,1,0:T(2,128)} copy(f32[1,2,32]{2,1,0:T(2,128)S(1)} %get-tuple-element.7) | data formatting | bytes 512
  42.6 0.6 %copy.17 = f32[1,2,32]{2,1,0:T(2,128)} copy(f32[1,2,32]{2,1,0:T(2,128)S(1)} %get-tuple-element.8) | data formatting | bytes 512
Async XLA Ops:
  0.6 0.8 %copy-start.5 = (s32[3,32]{1,0:T(4,128)S(1)}, s32[3,32]{1,0:T(4,128)}, u32[]{:S(2)}) copy-start(s32[3,32]{1,0:T(4,128)} %use_ref.1) | copy-start | bytes 1156
  0.6 0.8 %copy-start.6 = (s32[1,32]{1,0:T(1,128)S(1)}, s32[1,32]{1,0:T(1,128)}, u32[]{:S(2)}) copy-start(s32[1,32]{1,0:T(1,128)} %mask_ref.1) | copy-start | bytes 388
  1.4 1.0 %copy-start = (bf16[1,512,512]{2,1,0:T(8,128)(2,1)S(1)}, bf16[1,512,512]{2,1,0:T(8,128)(2,1)}, u32[]{:S(2)}) copy-start(bf16[1,512,512]{2,1,0:T(8,128)(2,1)} %tile_ref.1) | copy-start | bytes 1572868
  2.5 1.0 %copy-start.1 = (bf16[3,256,256]{2,1,0:T(8,128)(2,1)S(1)}, bf16[3,256,256]{2,1,0:T(8,128)(2,1)}, u32[]{:S(2)}) copy-start(bf16[3,256,256]{2,1,0:T(8,128)(2,1)} %constant.11.clone.second_ref) | copy-start | bytes 1179652
  3.5 1.0 %copy-start.2 = (bf16[768,256]{1,0:T(8,128)(2,1)S(1)}, bf16[768,256]{1,0:T(8,128)(2,1)}, u32[]{:S(2)}) copy-start(bf16[768,256]{1,0:T(8,128)(2,1)} %constant.10.clone.first_ref) | copy-start | bytes 1179652
  4.5 0.9 %copy-start.3 = (bf16[2,256,256]{2,1,0:T(8,128)(2,1)S(1)}, bf16[2,256,256]{2,1,0:T(8,128)(2,1)}, u32[]{:S(2)}) copy-start(bf16[2,256,256]{2,1,0:T(8,128)(2,1)} %constant.9.clone.cols_ref) | copy-start | bytes 786436
  5.4 0.8 %copy-start.4 = (bf16[128,128]{1,0:T(8,128)(2,1)S(1)}, bf16[128,128]{1,0:T(8,128)(2,1)}, u32[]{:S(2)}) copy-start(bf16[128,128]{1,0:T(8,128)(2,1)} %constant.8.clone.rows_ref) | copy-start | bytes 98308

commit v2 on v1

--- a/solution.py
+++ b/solution.py
@@ -12,6 +12,7 @@
 PATCH = 128
 HALF = PATCH // 2
 LEVELS = 3
+GROUP = 4
 MESH = pl.DeviceIdType.MESH
 
 
@@ -59,16 +60,28 @@
 
 
 def kernel(
-    n, tile_ref, place_ref, mask_ref, use_ref, rows_ref, cols_ref, first_ref, second_ref,
-    next_ref, skip_ref, pos_ref,
+    n, tile_hbm, place_hbm, mask_ref, use_ref, rows_hbm, cols_hbm, first_hbm, second_hbm,
+    out_ref,
+    tile_ref, place_ref, rows_ref, cols_ref, first_ref, second_ref, load_sem,
     wide, got, got_mask, own, totals, moments, mine, earlier,
-    tile_send, tile_recv, mask_send, mask_recv, flow_send, flow_recv,
+    tile_send, tile_recv, mask_send, mask_recv, flow_send, flow_recv, go,
 ):
     me = lax.axis_index("sec")
     grp = lax.axis_index("grp")
     patches = use_ref.shape[1]
     pairs = patches // 2
+    group = GROUP if pairs % GROUP == 0 else 2
     side = tile_ref.shape[1]
+
+    loads = [
+        pltpu.make_async_copy(src, dst, load_sem.at[i])
+        for i, (src, dst) in enumerate((
+            (tile_hbm, tile_ref), (place_hbm, place_ref), (rows_hbm, rows_ref),
+            (cols_hbm, cols_ref), (first_hbm, first_ref), (second_hbm, second_ref),
+        ))
+    ]
+    for load in loads:
+        load.start()
 
     barrier = pltpu.get_barrier_semaphore()
 
@@ -78,6 +91,7 @@
         return 0
 
     lax.fori_loop(1, n, greet, 0)
+    loads[0].wait()
     pl.semaphore_wait(barrier, n - 1)
 
     def tile_copy(gap):
@@ -94,16 +108,28 @@
             device_id=(grp, me - gap), device_id_type=MESH,
         )
 
+    odd = lax.rem(me, 2) == 1
+    relays = jnp.logical_and(odd, me + 1 < n)
+    skips = jnp.logical_and(odd, me >= 2)
+
+    def relay_copy():
+        return pltpu.make_async_remote_copy(
+            src_ref=got.at[0], dst_ref=got.at[1],
+            send_sem=tile_send.at[2], recv_sem=tile_recv.at[1],
+            device_id=(grp, me - 1), device_id_type=MESH,
+        )
+
     for gap in (1, 2):
         @pl.when(me >= gap)
         def _(gap=gap):
-            tile_copy(gap).start()
+            if gap == 1:
+                tile_copy(gap).start()
             mask_copy(gap).start()
 
     lane = lax.broadcasted_iota(jnp.int32, (PATCH, PATCH), 1)
 
     def patch(p):
-        row, col = place_ref[p, 0], place_ref[p, 1]
+        row, col = place_ref[0, p], place_ref[1, p]
         block = lax.div(col, PATCH)
         within = lax.rem(col, PATCH)
         a = wide[block, pl.ds(row, PATCH), :]
@@ -114,26 +140,26 @@
 
     def spectra(q):
         halves = []
-        for pair in (q, q + 1):
-            both = jnp.concatenate([patch(pair), patch(pair + pairs)], axis=1)
+        for pair in range(group):
+            both = jnp.concatenate([patch(q + pair), patch(q + pair + pairs)], axis=1)
             halves.append(dot(rows_ref[...], both).astype(jnp.bfloat16))
         u = dot(jnp.concatenate([h[:HALF] for h in halves], 0), cols_ref[0])
         v = dot(jnp.concatenate([h[HALF:] for h in halves], 0), cols_ref[1])
         plus, minus = (u + v).astype(jnp.bfloat16), (u - v).astype(jnp.bfloat16)
         return [
             jnp.concatenate([plus[HALF * i:HALF * (i + 1)], minus[HALF * i:HALF * (i + 1)]], 0)
-            for i in (0, 1)
+            for i in range(group)
         ]
 
     def own_quad(i, _):
-        for j, value in enumerate(spectra(2 * i)):
-            own[2 * i + j] = value
+        for j, value in enumerate(spectra(group * i)):
+            own[group * i + j] = value
         return 0
 
     sub = lax.broadcasted_iota(jnp.int32, (8, 2 * PATCH), 0).astype(jnp.float32)
 
     def pair_quad(i, _):
-        q = 2 * i
+        q = group * i
         real, imag = [], []
         for j, other in enumerate(spectra(q)):
             mine_ = own[q + j].astype(jnp.float32)
@@ -142,18 +168,22 @@
             br, bi = other[:, :PATCH], other[:, PATCH:]
             real.append((ar * br + ai * bi).astype(jnp.bfloat16))
             imag.append((ai * br - ar * bi).astype(jnp.bfloat16))
-        cross = jnp.concatenate(
-            [jnp.concatenate(real, 1), jnp.concatenate(imag, 1)], 0
-        )
+        halves = []
+        for j in range(0, group, 2):
+            cross = jnp.concatenate(
+                [jnp.concatenate(real[j:j + 2], 1), jnp.concatenate(imag[j:j + 2], 1)], 0
+            )
+            halves.append(dot(first_ref[...], cross).astype(jnp.bfloat16))
         for level in range(LEVELS):
-            half = dot(
-                first_ref[pl.ds(2 * PATCH * level, 2 * PATCH)], cross
-            ).astype(jnp.bfloat16)
-            for j in (0, 1):
-                lanes = slice(PATCH * j, PATCH * (j + 1))
-                both = jnp.concatenate([half[:PATCH, lanes], half[PATCH:, lanes]], 1)
-                correl = dot(both, second_ref[level])
-                weights = correl * correl
+            top = 2 * PATCH * level
+            both = jnp.concatenate([
+                jnp.concatenate([half[top:top + PATCH, lanes], half[top + PATCH:top + 2 * PATCH, lanes]], 1)
+                for half in halves for lanes in (slice(0, PATCH), slice(PATCH, 2 * PATCH))
+            ], 0)
+            correl = dot(both, second_ref[level])
+            for j in range(group):
+                weights = correl[PATCH * j:PATCH * (j + 1)]
+                weights = weights * weights
                 total = jnp.zeros((8, 2 * PATCH), jnp.float32)
                 moment = jnp.zeros((8, 2 * PATCH), jnp.float32)
                 for g in range(PATCH // 8):
@@ -165,9 +195,9 @@
                 total = jnp.sum(total, 0, keepdims=True)
                 moment = jnp.sum(moment, 0, keepdims=True)
                 for h in (0, 1):
-                    lanes_ = slice(PATCH * h, PATCH * (h + 1))
-                    totals[level, pl.ds(q + j + h * pairs, 1), :] = total[:, lanes_]
-                    moments[level, pl.ds(q + j + h * pairs, 1), :] = moment[:, lanes_]
+                    lanes = slice(PATCH * h, PATCH * (h + 1))
+                    totals[level, pl.ds(q + j + h * pairs, 1), :] = total[:, lanes]
+                    moments[level, pl.ds(q + j + h * pairs, 1), :] = moment[:, lanes]
         return 0
 
     position = lax.broadcasted_iota(jnp.int32, (8, PATCH), 1)
@@ -203,7 +233,16 @@
             wide[block] = plane[:, lanes].astype(jnp.float32)
 
     widen(tile_ref.at[0])
-    lax.fori_loop(0, pairs // 2, own_quad, 0)
+    for load in loads[1:]:
+        load.wait()
+    lax.fori_loop(0, pairs // group, own_quad, 0, unroll=2)
+
+    last_pair = jnp.logical_and(me == n - 2, jnp.logical_and(jnp.logical_not(odd), me >= 1))
+
+    @pl.when(last_pair)
+    def _():
+        tile_copy(1).wait_send()
+        pl.semaphore_signal(go, inc=1, device_id=(grp, me + 1), device_id_type=MESH)
 
     def flow_copy(other):
         return pltpu.make_async_remote_copy(
@@ -212,17 +251,25 @@
             device_id=(grp, other), device_id_type=MESH,
         )
 
-    for gap, out in ((1, next_ref), (2, skip_ref)):
+    for gap, out in ((1, out_ref.at[0]), (2, out_ref.at[1])):
         @pl.when(me + gap < n)
         def _(gap=gap, out=out):
             tile_copy(gap).wait_recv()
+            if gap == 1:
+                pl.when(relays)(lambda: relay_copy().start())
+                pl.when(skips)(lambda: tile_copy(2).start())
             mask_copy(gap).wait_recv()
             widen(got.at[gap - 1])
-            lax.fori_loop(0, pairs // 2, pair_quad, 0)
+            lax.fori_loop(0, pairs // group, pair_quad, 0, unroll=2)
             out[0] = flow(gap)
 
         @pl.when(me + gap >= n)
-        def _(out=out):
+        def _(gap=gap, out=out):
+            if gap == 1:
+                @pl.when(skips)
+                def _():
+                    pl.semaphore_wait(go, 1)
+                    tile_copy(2).start()
             out[...] = jnp.zeros_like(out)
 
         if gap == 1:
@@ -243,7 +290,7 @@
         return state + earlier[t]
 
     before = lax.fori_loop(0, me, arrived, jnp.zeros(mine.shape, jnp.float32))
-    pos_ref[0] = before + mine[...]
+    out_ref[2, 0] = before + mine[...]
 
     def sent(other, _):
         flow_copy(other).wait_send()
@@ -253,23 +300,31 @@
     for gap in (1, 2):
         @pl.when(me >= gap)
         def _(gap=gap):
-            tile_copy(gap).wait_send()
+            if gap == 1:
+                pl.when(jnp.logical_not(last_pair))(lambda: tile_copy(1).wait_send())
             mask_copy(gap).wait_send()
+    pl.when(relays)(lambda: relay_copy().wait_send())
+    pl.when(skips)(lambda: tile_copy(2).wait_send())
 
 
 def on_device(n, section_tile, placement, tissue_mask, level_use):
     side = section_tile.shape[1]
     patches = placement.shape[0]
-    out = jax.ShapeDtypeStruct((1, 2, patches), jnp.float32)
+    out = jax.ShapeDtypeStruct((3, 1, 2, patches), jnp.float32)
     vmem = pl.BlockSpec(memory_space=pltpu.VMEM)
-    smem = pl.BlockSpec(memory_space=pltpu.SMEM)
     dma = pltpu.SemaphoreType.DMA
-    return pl.pallas_call(
+    consts = [jnp.asarray(t) for t in tables()]
+    anywhere = pl.BlockSpec(memory_space=pl.ANY)
+    flows = pl.pallas_call(
         functools.partial(kernel, n),
-        out_shape=(out, out, out),
-        in_specs=[vmem, smem] + [vmem] * 6,
-        out_specs=(vmem, vmem, vmem),
+        out_shape=out,
+        in_specs=[anywhere] * 2 + [vmem] * 2 + [anywhere] * 4,
+        out_specs=vmem,
         scratch_shapes=[
+            pltpu.VMEM(section_tile.shape, section_tile.dtype),
+            pltpu.SMEM((2, patches), placement.dtype),
+            *[pltpu.VMEM(t.shape, t.dtype) for t in consts],
+            dma((6,)),
             pltpu.VMEM((side // PATCH, side, PATCH), jnp.float32),
             pltpu.VMEM((2, side, side), jnp.bfloat16),
             pltpu.VMEM((2, 1, patches), jnp.int32),
@@ -278,12 +333,13 @@
             pltpu.VMEM((LEVELS, patches, PATCH), jnp.float32),
             pltpu.VMEM((2, patches), jnp.float32),
             pltpu.VMEM((n, 2, patches), jnp.float32),
-            dma((2,)), dma((2,)), dma((2,)), dma((2,)), dma((n,)), dma((n,)),
+            dma((3,)), dma((2,)), dma((2,)), dma((2,)), dma((n,)), dma((n,)), pltpu.SemaphoreType.REGULAR,
         ],
         compiler_params=pltpu.CompilerParams(
-            collective_id=0, has_side_effects=True, vmem_limit_bytes=40 * 2**20
+            collective_id=0, has_side_effects=True, vmem_limit_bytes=56 * 2**20
         ),
-    )(section_tile, placement, tissue_mask, level_use, *[jnp.asarray(t) for t in tables()])
+    )(section_tile, placement.T, tissue_mask, level_use, *consts)
+    return flows[0], flows[1], flows[2]
 
 
 def solution(mesh):

time: 43.6 us -> 28.9 us (0.66)
  Pallas kernels: 35.3 us -> 26.9 us
  local copies, waits for them, and re-layouts: 7.2 us -> 1.25 us
    pallas_call x1, Pallas kernels: 35.3 us -> 26.9 us  [on_device(): pl.pallas_call(functools.partial(kernel, n), out_shape=out, in_specs=[any...]
    unnamed x18 -> x0, local copies, waits for them, and re-layouts: 7.2 us -> none
    squeeze x0 -> x1, local copies, waits for them, and re-layouts: none -> 1.25 us  [on_device(): return (flows[0], flows[1], flows[2])]
where the time goes in v2:
time: 28.9 us; the launch traced here: 28.8 us
  Pallas kernels  26.9 us (93%)
  local copies, waits for them, and re-layouts  1.25 us (4%)
  between operations  0.64 us (2%)
    pallas_call x1, Pallas kernels, on_device(): pl.pallas_call(functools.partial(kernel, n), out_shape=out, in_specs=[any...  26.9 us
    squeeze x1, local copies, waits for them, and re-layouts, on_device(): return (flows[0], flows[1], flows[2])  1.25 us

profile of v2, /device:TPU:1, one launch (start us, length us, event | category | flops | bytes accessed | tf_op | source)
XLA Modules:
  0.0 28.8 jit_solution(2829132668789851954)
XLA Ops:
  0.6 26.9 %shard_map.103 = f32[3,1,2,32]{3,2,1,0:T(2,128)} custom-call(bf16[1,512,512]{2,1,0:T(8,128)(2,1)} %tile_hbm.1, s32[2,32]{1,0:T(2,128)} %bitcast.7, s32[1,32]{1,0:T(1,128)} %mask_ref.1, s32[3,32]{1,0:T(4,128)} %use_ref.1, bf16[128,128]{1,0:T(8,128)(2,1)} %constant.8.clone.rows_hbm, bf16[2,256,256]{2,1,0:T(8,128)(2,1)} %constant.9.clone.cols_hbm, ...), custom_call_target="tpu_custom_call" | custom-call | tf_op jit(solution)/shard_map/pallas_call | solution.py:318
  27.5 1.2 %slice_bitcast_fusion = (f32[1,2,32]{2,1,0:T(2,128)}, f32[1,2,32]{2,1,0:T(2,128)}, f32[1,2,32]{2,1,0:T(2,128)}) fusion(f32[3,1,2,32]{3,2,1,0:T(2,128)} %shard_map.103), kind=kLoop, calls=%fused_computation | loop fusion | bytes 1536 | tf_op jit(solution)/shard_map/squeeze | solution.py:342

commit v3 on v2

--- a/solution.py
+++ b/solution.py
@@ -64,7 +64,7 @@
     out_ref,
     tile_ref, place_ref, rows_ref, cols_ref, first_ref, second_ref, load_sem,
     wide, got, got_mask, own, totals, moments, mine, earlier,
-    tile_send, tile_recv, mask_send, mask_recv, flow_send, flow_recv, go,
+    tile_send, tile_recv, mask_send, mask_recv, flow_send, flow_recv, go, here,
 ):
     me = lax.axis_index("sec")
     grp = lax.axis_index("grp")
@@ -85,14 +85,32 @@
 
     barrier = pltpu.get_barrier_semaphore()
 
-    def greet(step, _):
-        other = lax.rem(me + step, n)
-        pl.semaphore_signal(barrier, inc=1, device_id=(grp, other), device_id_type=MESH)
-        return 0
-
-    lax.fori_loop(1, n, greet, 0)
+    def around(distance, semaphore):
+        for other, there in ((me - distance, me >= distance), (me + distance, me + distance < n)):
+            @pl.when(there)
+            def _(other=other):
+                pl.semaphore_signal(semaphore, inc=1, device_id=(grp, other), device_id_type=MESH)
+
+    def await_around(distance, semaphore):
+        peers = (me >= distance).astype(jnp.int32) + (me + distance < n).astype(jnp.int32)
+        pl.semaphore_wait(semaphore, peers)
+
+    distances = []
+    while 2 ** (len(distances) + 1) < n:
+        distances.append(2 ** (len(distances) + 1))
+
+    def say(turn):
+        if turn < len(distances):
+            around(distances[turn], here.at[turn])
+
+    def hear(turn):
+        if turn < len(distances):
+            await_around(distances[turn], here.at[turn])
+
+    around(1, barrier)
+    around(2, barrier)
     loads[0].wait()
-    pl.semaphore_wait(barrier, n - 1)
+    pl.semaphore_wait(barrier, jnp.minimum(me, 2) + jnp.minimum(n - 1 - me, 2))
 
     def tile_copy(gap):
         return pltpu.make_async_remote_copy(
@@ -125,6 +143,7 @@
             if gap == 1:
                 tile_copy(gap).start()
             mask_copy(gap).start()
+    say(0)
 
     lane = lax.broadcasted_iota(jnp.int32, (PATCH, PATCH), 1)
 
@@ -244,6 +263,18 @@
         tile_copy(1).wait_send()
         pl.semaphore_signal(go, inc=1, device_id=(grp, me + 1), device_id_type=MESH)
 
+    hear(0)
+    say(1)
+
+    @pl.when(me + 1 < n)
+    def _():
+        tile_copy(1).wait_recv()
+        pl.when(relays)(lambda: relay_copy().start())
+        pl.when(skips)(lambda: tile_copy(2).start())
+
+    hear(1)
+    say(2)
+
     def flow_copy(other):
         return pltpu.make_async_remote_copy(
             src_ref=mine, dst_ref=earlier.at[me],
@@ -254,10 +285,8 @@
     for gap, out in ((1, out_ref.at[0]), (2, out_ref.at[1])):
         @pl.when(me + gap < n)
         def _(gap=gap, out=out):
-            tile_copy(gap).wait_recv()
-            if gap == 1:
-                pl.when(relays)(lambda: relay_copy().start())
-                pl.when(skips)(lambda: tile_copy(2).start())
+            if gap == 2:
+                tile_copy(gap).wait_recv()
             mask_copy(gap).wait_recv()
             widen(got.at[gap - 1])
             lax.fori_loop(0, pairs // group, pair_quad, 0, unroll=2)
@@ -274,6 +303,9 @@
 
         if gap == 1:
             mine[...] = out[0]
+            for turn in range(2, len(distances)):
+                hear(turn)
+                say(turn + 1)
 
             def send(other, _):
                 flow_copy(other).start()
@@ -334,6 +366,7 @@
             pltpu.VMEM((2, patches), jnp.float32),
             pltpu.VMEM((n, 2, patches), jnp.float32),
             dma((3,)), dma((2,)), dma((2,)), dma((2,)), dma((n,)), dma((n,)), pltpu.SemaphoreType.REGULAR,
+            pltpu.SemaphoreType.REGULAR((max(1, n.bit_length()),)),
         ],
         compiler_params=pltpu.CompilerParams(
             collective_id=0, has_side_effects=True, vmem_limit_bytes=56 * 2**20

time: 28.9 us -> 27 us (0.934)
  Pallas kernels: 26.9 us -> 24.9 us
    pallas_call x1, Pallas kernels: 26.9 us -> 24.9 us  [on_device(): pl.pallas_call(functools.partial(kernel, n), out_shape=out, in_specs=[any...]
where the time goes in v3:
time: 27 us; the launch traced here: 26.8 us
  Pallas kernels  24.9 us (92%)
  local copies, waits for them, and re-layouts  1.25 us (5%)
  between operations  0.64 us (2%)
    pallas_call x1, Pallas kernels, on_device(): pl.pallas_call(functools.partial(kernel, n), out_shape=out, in_specs=[any...  24.9 us
    squeeze x1, local copies, waits for them, and re-layouts, on_device(): return (flows[0], flows[1], flows[2])  1.25 us

profile of v3, /device:TPU:1, one launch (start us, length us, event | category | flops | bytes accessed | tf_op | source)
XLA Modules:
  0.0 26.8 jit_solution(10100797132051006509)
XLA Ops:
  0.6 24.9 %shard_map.103 = f32[3,1,2,32]{3,2,1,0:T(2,128)} custom-call(bf16[1,512,512]{2,1,0:T(8,128)(2,1)} %tile_hbm.1, s32[2,32]{1,0:T(2,128)} %bitcast.7, s32[1,32]{1,0:T(1,128)} %mask_ref.1, s32[3,32]{1,0:T(4,128)} %use_ref.1, bf16[128,128]{1,0:T(8,128)(2,1)} %constant.8.clone.rows_hbm, bf16[2,256,256]{2,1,0:T(8,128)(2,1)} %constant.9.clone.cols_hbm, ...), custom_call_target="tpu_custom_call" | custom-call | tf_op jit(solution)/shard_map/pallas_call | solution.py:350
  25.5 1.2 %slice_bitcast_fusion = (f32[1,2,32]{2,1,0:T(2,128)}, f32[1,2,32]{2,1,0:T(2,128)}, f32[1,2,32]{2,1,0:T(2,128)}) fusion(f32[3,1,2,32]{3,2,1,0:T(2,128)} %shard_map.103), kind=kLoop, calls=%fused_computation | loop fusion | bytes 1536 | tf_op jit(solution)/shard_map/squeeze | solution.py:375
